TPU v7x, 32 devices: a whole 2x2x4 slice. The times are simulated.
32 devices in a mesh: slab: 8 (over z, y), tile: 4 (over x, core).
Axes of the slice: x: 2, y: 2, z: 4, core: 2. Of those that a mesh axis runs over, the one named last changes fastest.
Arguments:
- brdf_bins: bfloat16 [3, 40, 180, 2048], P(None, 'slab', None, 'tile'), may hold values from -6 to 6
- diffusion: float32 [3, 40, 180], replicated, may hold values from 0.01 to 0.08
- valid_mask: int32 [40, 180], P('slab'), may hold values 0 or 1
- tile_owner: int32 [10], replicated, may hold values from 0 to 3, as said below
Outputs:
- owned_tiles: float32 [24, 512, 512], P('tile', 'slab')
Inputs may be any that keep to these rules, and one draw needn't show every extreme that they name: `tile_owner`: one owner holds exactly 6 tiles and none more; no owner holds more than 2 tiles of one tile row or of one tile column, and some owner holds 2 of some row and 2 of some column; counts are uneven.
All inputs are finite; a program needn't handle non-finite values. No bound on the sum of `valid_mask` on one device may be relied on, other than what follows from the above.
Results may differ from a plain program's by a relative error of at most 0.0003.
Values may be sent and summed in bfloat16 or wider, within the bound.
A program may use at most 128 MiB of HBM per device.

v0:
```python
import math

import jax
import jax.numpy as jnp
import numpy as np
from jax import lax
from jax.sharding import PartitionSpec as P

SWEEPS = 2


def padded_2(cells, sides, width):
    for axis, dim in sides:
        count = lax.axis_size(axis)
        ends = count - 1
        head = lax.slice_in_dim(cells, 0, width, axis=dim)
        tail = lax.slice_in_dim(cells, cells.shape[dim] - width, cells.shape[dim], axis=dim)
        cells = jnp.concatenate(
            [
                lax.ppermute(tail, axis, [(i, (i + 1) % count) for i in range(ends)]),
                cells,
                lax.ppermute(head, axis, [((i + 1) % count, i) for i in range(ends)]),
            ],
            axis=dim,
        )
    return cells


def stencil(padded, diffusion_rows):
    center = padded[:, 1:-1]
    pad_chan = jnp.pad(center, ((1, 1), (0, 0), (0, 0), (0, 0)))
    neighbours = padded[:, 2:] + padded[:, :-2] + pad_chan[2:] + pad_chan[:-2]
    neighbours = neighbours + jnp.roll(center, 1, 2) + jnp.roll(center, -1, 2)
    return center + diffusion_rows[..., None] * (neighbours - 6.0 * center)


def contract_rows(left_cols, right_cols):
    return lax.dot_general(
        left_cols, right_cols, (((0,), (0,)), ((), ())), preferred_element_type=jnp.float32
    )


def on_device(brdf_bins, diffusion, valid_mask, tile_owner):
    n_tiles = lax.axis_size("tile")
    my_tile = lax.axis_index("tile")
    slab_width = brdf_bins.shape[1]
    slab_start = lax.axis_index("slab") * slab_width
    extended = padded_2(brdf_bins, (("slab", 1),), SWEEPS)
    field = extended.astype(jnp.float32)
    margin_diffusion = jnp.pad(diffusion, ((0, 0), (SWEEPS - 1, SWEEPS - 1), (0, 0)))
    for sweep_idx in range(SWEEPS):
        span_rows = slab_width + 2 * (SWEEPS - 1 - sweep_idx)
        local_diffusion = lax.dynamic_slice_in_dim(
            margin_diffusion, slab_start + sweep_idx, span_rows, 1
        )
        field = stencil(field, local_diffusion)
    smooth = (field * valid_mask[None, :, :, None].astype(jnp.float32)).astype(jnp.bfloat16)
    flat_rows = smooth.reshape(-1, smooth.shape[-1])
    tile_width = flat_rows.shape[1]
    gram_scale = 1.0 / math.sqrt(flat_rows.shape[0] * lax.axis_size("slab"))
    row_tile, col_tile = np.triu_indices(n_tiles)
    n_upper = row_tile.shape[0]
    column_block = contract_rows(lax.all_gather(flat_rows, "tile", axis=1, tiled=True), flat_rows)
    tile_slots = column_block.reshape(n_tiles, tile_width, tile_width)
    slot_table = np.full((n_tiles, n_tiles), -1, np.int32)
    slot_table[col_tile, row_tile] = np.arange(n_upper, dtype=np.int32)
    reduced = lax.psum_scatter(tile_slots, "slab", scatter_dimension=1, tiled=True) * gram_scale
    my_upper = jnp.asarray(slot_table)[my_tile]
    has_upper = my_upper >= 0
    safe_upper = jnp.clip(my_upper, 0, n_upper - 1)
    destination = jnp.where(has_upper, tile_owner[safe_upper], -1)
    position = jnp.arange(n_upper, dtype=jnp.int32)
    same_owner = tile_owner[None, :] == tile_owner[:, None]
    before = same_owner & (position[None, :] < position[:, None])
    rank_in = jnp.sum(before.astype(jnp.int32), axis=1)
    to_dest = (destination[None, :] == jnp.arange(n_tiles, dtype=jnp.int32)[:, None]).astype(
        jnp.float32
    )
    outgoing = to_dest[:, :, None, None] * reduced[None]
    received = lax.all_to_all(outgoing, "tile", split_axis=0, concat_axis=0, tiled=True)
    received = received.reshape(n_tiles * n_tiles, received.shape[2], received.shape[3])
    recv_index = jnp.asarray((col_tile * n_tiles + row_tile).astype(np.int32))
    cap_slots = 2 * ((n_upper + n_tiles - 1) // n_tiles)
    slot_ids = jnp.arange(cap_slots, dtype=jnp.int32)
    chosen = (tile_owner[None, :] == my_tile) & (rank_in[None, :] == slot_ids[:, None])
    source_idx = jnp.sum(jnp.where(chosen, recv_index[None, :], 0), axis=1).astype(jnp.int32)
    filled = jnp.any(chosen, axis=1)
    picked = jnp.take(received, source_idx, axis=0)
    return jnp.where(filled[:, None, None], picked, 0.0)


def solution(mesh):
    in_specs = (P(None, "slab", None, "tile"), P(), P("slab", None), P())
    out_specs = P("tile", "slab", None)
    return jax.shard_map(
        on_device, mesh=mesh, in_specs=in_specs, out_specs=out_specs, check_vma=False
    )
```

profile of v0, /device:TPU:23, one launch (start us, length us, event | category | flops | bytes accessed | tf_op | source)
XLA Modules:
  0.0 335.4 jit_solution(14037890006734984520)
XLA Ops:
  6.5 3.3 fusion.26
  9.8 3.1 collective-permute-start
  12.9 2.1 collective-permute-start.1
  15.1 1.3 convert_element_type.29
  16.4 1.4 pad_dynamic-slice_fusion.1
  17.8 0.8 pad_dynamic-slice_fusion
  18.6 43.4 %collective-permute-done = bf16[3,2,180,512]{3,2,1,0:T(8,128)(2,1)} collective-permute-done((bf16[3,2,180,512]{3,2,1,0:T(8,128)(2,1)}, bf16[3,2,180,512]{3,2,1,0:T(8,128)(2,1)}, u32[]{:S(2)}, u32[]{:S(2)}) %collective-permute-start) | collective-permute-done | bytes 1105952 | tf_op jit(solution)/shard_map/ppermute | solution.py:20
  62.0 2.1 maximum_convert_fusion
  64.1 6.4 %fusion.23 = (f32[3,7,179,512]{3,2,1,0:T(8,128)}, f32[3,7,179,512]{3,2,1,0:T(8,128)}) fusion(f32[3,9,180,512]{3,2,1,0:T(8,128)S(1)} %maximum_convert_fusion), kind=kLoop, calls=%fused_computation.53 | loop fusion | bytes 30793728 | tf_op jit(solution)/shard_map/jit(_roll_static)/slice | solution.py:33
  70.5 4.1 %slice.100 = f32[3,7,180,512]{3,2,1,0:T(8,128)} slice(f32[3,9,180,512]{3,2,1,0:T(8,128)S(1)} %maximum_convert_fusion), slice={[0:3], [1:8], [0:180], [0:512]} | slice | bytes 15482880 | tf_op jit(solution)/shard_map/slice | solution.py:30
  74.6 1.5 maximum_convert_fusion.1
  76.0 14.4 %fusion.6 = f32[3,7,180,512]{3,2,1,0:T(8,128)} fusion(f32[3,7,180,512]{3,2,1,0:T(8,128)} %slice.100, f32[3,9,180,512]{3,2,1,0:T(8,128)S(1)} %maximum_convert_fusion, f32[3,7,179,512]{3,2,1,0:T(8,128)} %get-tuple-element.6, f32[3,7,1,512]{3,2,1,0:T(1,128)} %get-tuple-element.12, f32[3,7,1,512]{3,2,1,0:T(1,128)S(1)} %get-tuple-element.11, ...), kind=kLoop, calls=%fused_computation.12 | loop fusion | flops 21288960 | bytes 46463760 | tf_op jit(solution)/shard_map/add | solution.py:34
  90.4 10.6 %fusion.24 = (f32[3,5,179,512]{3,2,1,0:T(8,128)}, f32[3,5,179,512]{3,2,1,0:T(8,128)}) fusion(f32[3,7,180,512]{3,2,1,0:T(8,128)} %fusion.6), kind=kLoop, calls=%fused_computation.54 | loop fusion | bytes 21995520 | tf_op jit(solution)/shard_map/jit(_roll_static)/slice | solution.py:33
  101.1 2.6 slice-done
  103.7 1.7 copy-done.2
  105.4 6.4 %fusion.15 = bf16[3,5,180,512]{3,2,1,0:T(8,128)(2,1)S(1)} fusion(f32[3,5,180,512]{3,2,1,0:T(8,128)S(1)} %slice-done, f32[3,7,180,512]{3,2,1,0:T(8,128)S(1)} %copy-done.1, f32[3,5,179,512]{3,2,1,0:T(8,128)} %get-tuple-element.8, f32[3,5,1,512]{3,2,1,0:T(1,128)S(1)} %get-tuple-element.10, f32[3,5,1,512]{3,2,1,0:T(1,128)S(1)} %get-tuple-element.9, ...), kind=kLoop, calls=%fused_computation.22 | loop fusion | flops 17971200 | bytes 30427200 | tf_op jit(solution)/shard_map/convert_element_type | solution.py:57
  111.8 2.0 reshape.82
  113.8 4.5 %copy.9 = bf16[2700,512]{0,1:T(8,128)(2,1)} copy(bf16[2700,512]{1,0:T(8,128)(2,1)} %reshape.82) | data formatting | bytes 5529600 | tf_op jit(solution)/shard_map/reshape | solution.py:58
  118.4 2.0 reshape.100
  120.4 75.6 %all-gather.2.cloned.1.call-done = bf16[2700,2048]{0,1:T(8,128)(2,1)} async-done(((bf16[2700,512]{0,1:T(8,128)(2,1)}), bf16[2700,2048]{0,1:T(8,128)(2,1)}) %all-gather.2.cloned.1.call-update) | async-done | bytes 11059216 | tf_op jit(solution)/shard_map/all_gather | solution.py:63
  196.0 11.1 %fusion.27 = f32[4,512,512]{2,1,0:T(8,128)} fusion(bf16[4,512,2700]{2,1,0:T(8,128)(2,1)} %bitcast.19, bf16[2700,512,1]{1,0,2:T(8,128)(2,1)} %reshape.100), kind=kOutput, calls=%fused_computation.57 | convolution fusion | flops 5662310400 | bytes 18018304 | tf_op jit(solution)/shard_map/dot_general | solution.py:38
  207.2 0.6 gather_fusion
  207.9 88.1 %reduce-scatter.2.cloned.1.call-done = f32[4,64,512]{2,1,0:T(8,128)} async-done(((f32[4,512,512]{2,1,0:T(8,128)}), f32[4,64,512]{2,1,0:T(8,128)}) %reduce-scatter.2.cloned.1.call-update) | async-done | bytes 524304 | tf_op jit(solution)/shard_map/reduce_scatter | solution.py:67
  295.9 1.1 broadcast_multiply_fusion.1
  297.0 1.7 broadcast_multiply_fusion
  298.7 4.4 %all-to-all-start = ((f32[4,4,64,512]{3,2,1,0:T(8,128)}), f32[4,4,64,512]{3,2,1,0:T(8,128)S(1)}, u32[]{:S(2)}, u32[]{:S(2)}) async-start(f32[4,4,64,512]{3,2,1,0:T(8,128)} %broadcast_multiply_fusion), calls=%async_computation.1 | async-start | bytes 4194304 | tf_op jit(solution)/shard_map/all_to_all | solution.py:80
  303.1 0.2 convert_reduce_fusion
  303.3 0.1 select_reduce_fusion
  303.4 0.1 fusion.18
  303.5 23.3 %all-to-all-done = f32[4,4,64,512]{3,2,1,0:T(8,128)S(1)} async-done(((f32[4,4,64,512]{3,2,1,0:T(8,128)}), f32[4,4,64,512]{3,2,1,0:T(8,128)S(1)}, u32[]{:S(2)}, u32[]{:S(2)}) %all-to-all-start) | async-done | bytes 2097184 | tf_op jit(solution)/shard_map/all_to_all | solution.py:80
  326.9 0.6 gather_fusion.1
  327.5 1.0 select_select_fusion
  (28 shorter events, 0.2 us)
Async XLA Ops:
  6.5 55.5 %copy-start.3 = (bf16[3,5,180,512]{3,2,1,0:T(8,128)(2,1)S(1)}, bf16[3,5,180,512]{3,2,1,0:T(8,128)(2,1)}, u32[]{:S(2)}) copy-start(bf16[3,5,180,512]{3,2,1,0:T(8,128)(2,1)} %param.6) | copy-start | bytes 8294404
  6.5 189.4 %all-gather.2.cloned.1.call-start = ((), (), s32[]{:S(2)}) async-start(), calls=%async_computation.2 | async-start | bytes 14417920 | tf_op jit(solution)/shard_map/all_gather | solution.py:63
  9.8 52.2 %collective-permute-start = (bf16[3,2,180,512]{3,2,1,0:T(8,128)(2,1)}, bf16[3,2,180,512]{3,2,1,0:T(8,128)(2,1)}, u32[]{:S(2)}, u32[]{:S(2)}) collective-permute-start(bf16[3,2,180,512]{3,2,1,0:T(8,128)(2,1)} %get-tuple-element.13), channel_id=1, source_target_pairs={{0,4},{4,8},{8,12},{12,16},{16,20},{20,24},{24,28},{1,5},{5,9},{9,... | collective-permute-start | bytes 3317768 | tf_op jit(solution)/shard_map/ppermute | solution.py:20
  12.9 49.1 %collective-permute-start.1 = (bf16[3,2,180,512]{3,2,1,0:T(8,128)(2,1)}, bf16[3,2,180,512]{3,2,1,0:T(8,128)(2,1)}, u32[]{:S(2)}, u32[]{:S(2)}) collective-permute-start(bf16[3,2,180,512]{3,2,1,0:T(8,128)(2,1)} %get-tuple-element.14), channel_id=1, source_target_pairs={{4,0},{8,4},{12,8},{16,12},{20,16},{24,20},{28,24},{5,1},{9,5},{13... | collective-permute-start | bytes 3317768 | tf_op jit(solution)/shard_map/ppermute | solution.py:22
  90.4 10.6 %copy-start.1 = (f32[3,7,180,512]{3,2,1,0:T(8,128)S(1)}, f32[3,7,180,512]{3,2,1,0:T(8,128)}, u32[]{:S(2)}) copy-start(f32[3,7,180,512]{3,2,1,0:T(8,128)} %fusion.6) | copy-start | bytes 23224324
  90.4 10.7 %copy-start.4 = (f32[5,180]{1,0:T(8,128)S(1)}, f32[5,180]{1,0:T(8,128)}, u32[]{:S(2)}) copy-start(f32[5,180]{1,0:T(8,128)} %convert_element_type.29) | copy-start | bytes 10804
  101.1 2.6 slice-start
  101.1 4.3 %copy-start.2 = (f32[3,5,179,512]{3,2,1,0:T(8,128)S(1)}, f32[3,5,179,512]{3,2,1,0:T(8,128)}, u32[]{:S(2)}) copy-start(f32[3,5,179,512]{3,2,1,0:T(8,128)} %get-tuple-element.7) | copy-start | bytes 16496644
  118.4 177.6 %reduce-scatter.2.cloned.1.call-start = ((), (), s32[]{:S(2)}) async-start(), calls=%async_computation.3 | async-start | bytes 4718592 | tf_op jit(solution)/shard_map/reduce_scatter | solution.py:67
  196.0 11.2 %copy-start.6 = (s32[4,4]{1,0:T(4,128)S(1)}, s32[4,4]{1,0:T(4,128)}, u32[]{:S(2)}) copy-start(s32[4,4]{1,0:T(4,128)} %constant.57.clone) | copy-start | bytes 196
  196.0 11.2 %copy-start = (s32[10]{0:T(128)S(1)}, s32[10]{0:T(128)}, u32[]{:S(2)}) copy-start(s32[10]{0:T(128)} %param.9) | copy-start | bytes 124
  207.1 96.1 %copy-start.5 = (s32[10]{0:T(128)S(1)}, s32[10]{0:T(128)}, u32[]{:S(2)}) copy-start(s32[10]{0:T(128)} %constant.58.clone) | copy-start | bytes 124
  298.7 28.2 %all-to-all-start = ((f32[4,4,64,512]{3,2,1,0:T(8,128)}), f32[4,4,64,512]{3,2,1,0:T(8,128)S(1)}, u32[]{:S(2)}, u32[]{:S(2)}) async-start(f32[4,4,64,512]{3,2,1,0:T(8,128)} %broadcast_multiply_fusion), calls=%async_computation.1 | async-start | bytes 4194304 | tf_op jit(solution)/shard_map/all_to_all | solution.py:80
Sparse Core Ops, SparseCore 0:
  118.5 77.4 all-gather.1
  207.3 88.6 reduce-scatter.1
where the time goes:
time: 339 us; the launch traced here: 335 us
  waiting for transfers between devices  230 us (68%)
  local copies, waits for them, and re-layouts  40.6 us (12%)
  other arithmetic  29.9 us (9%)
  between operations  13.5 us (4%)
  matrix products  11.1 us (3%)
  starting transfers between devices  9.69 us (3%)
    reduce_scatter x1, waiting for transfers between devices, on_device(): lax.psum_scatter(tile_slots, 'slab', scatter_dimension=1, tiled=True)  88.1 us
    all_gather x1, waiting for transfers between devices, on_device(): lax.all_gather(flat_rows, 'tile', axis=1, tiled=True)  75.6 us
    ppermute x1, waiting for transfers between devices, padded_2(): lax.ppermute(tail, axis, [(i, (i + 1) % count) for i in range(ends)])  43.4 us
    all_to_all x1, waiting for transfers between devices, on_device(): lax.all_to_all(outgoing, 'tile', split_axis=0, concat_axis=0, tiled=True)  23.3 us
    slice x3, local copies, waits for them, and re-layouts, stencil(): neighbours = neighbours + jnp.roll(center, 1, 2) + jnp.roll(center, -1, 2)  17.1 us
    add x1, other arithmetic, stencil(): return center + diffusion_rows[..., None] * (neighbours - 6.0 * center)  14.4 us
    dot_general x1, matrix products, contract_rows(): lax.dot_general(left_cols, right_cols, (((0,), (0,)), ((), ())), preferre...  11.1 us
    reshape x3, local copies, waits for them, and re-layouts, on_device(): flat_rows = smooth.reshape(-1, smooth.shape[-1])  8.49 us
  transfers between devices with their start and end apart: 5, of which 4 were waited for; matrix products, arithmetic and copies ran while one was open for 2% of the time, Pallas kernels for 0%

commit v1 on v0

--- a/solution.py
+++ b/solution.py
@@ -1,9 +1,12 @@
+import functools
 import math
 
 import jax
 import jax.numpy as jnp
 import numpy as np
 from jax import lax
+from jax.experimental import pallas as pl
+from jax.experimental.pallas import tpu as pltpu
 from jax.sharding import PartitionSpec as P
 
 SWEEPS = 2
@@ -89,9 +92,358 @@
     return jnp.where(filled[:, None, None], picked, 0.0)
 
 
+MESH = pl.DeviceIdType.MESH
+LANES = 128
+HALF = 96
+OFF = 8
+SEGS = ((0, 512), (512, 256), (768, 512), (1280, 512))
+
+
+def contract(left, right):
+    return lax.dot_general(
+        left, right, (((0,), (0,)), ((), ())), preferred_element_type=jnp.float32
+    )
+
+
+def gram_kernel(
+    scale, bins, diff, mask, out, lo, hi, f0, f1, smooth, partner, across, gram, ybuf, zbuf,
+    halo_send, halo_recv, core_send, core_recv, x_send, x_recv, y_send, y_recv, z_send, z_recv,
+    g_send, g_recv, gx_send, gx_recv, gf_send, gf_recv,
+):
+    slab = lax.axis_index("slab")
+    tile = lax.axis_index("tile")
+    z = slab // 2
+    y = lax.rem(slab, 2)
+    chip = tile // 2
+    core = lax.rem(tile, 2)
+    core_peer = 2 * chip + 1 - core
+    x_peer = lax.rem(tile + 2, 4)
+    chans, rows, phis, width = bins.shape
+    n_chunk = width // LANES
+    groups = chans * rows
+    half_rows = groups * HALF
+
+    barrier = pltpu.get_barrier_semaphore()
+    for step in range(1, 8):
+        pl.semaphore_signal(
+            barrier, inc=1, device_id=(lax.rem(slab + step, 8), tile), device_id_type=MESH
+        )
+    for other in (core_peer, x_peer):
+        pl.semaphore_signal(barrier, inc=1, device_id=(slab, other), device_id_type=MESH)
+    pl.semaphore_wait(barrier, 9)
+
+    def lanes_of(m):
+        return pl.ds(pl.multiple_of(m * LANES, LANES), LANES)
+
+    def halo_up(m):
+        return pltpu.make_async_remote_copy(
+            src_ref=bins.at[:, pl.ds(rows - 2, 2), :, lanes_of(m)],
+            dst_ref=lo.at[:, :, :, lanes_of(m)],
+            send_sem=halo_send.at[0, m], recv_sem=halo_recv.at[0, m],
+            device_id=(jnp.minimum(slab + 1, 7), tile), device_id_type=MESH,
+        )
+
+    def halo_down(m):
+        return pltpu.make_async_remote_copy(
+            src_ref=bins.at[:, pl.ds(0, 2), :, lanes_of(m)],
+            dst_ref=hi.at[:, :, :, lanes_of(m)],
+            send_sem=halo_send.at[1, m], recv_sem=halo_recv.at[1, m],
+            device_id=(jnp.maximum(slab - 1, 0), tile), device_id_type=MESH,
+        )
+
+    for m in range(n_chunk):
+        @pl.when(slab < 7)
+        def _():
+            halo_up(m).start()
+
+        @pl.when(slab > 0)
+        def _():
+            halo_down(m).start()
+
+    @pl.when(slab == 0)
+    def _():
+        lo[...] = jnp.zeros_like(lo)
+
+    @pl.when(slab == 7)
+    def _():
+        hi[...] = jnp.zeros_like(hi)
+
+    for ref in (f0, f1):
+        for c in range(ref.shape[0]):
+            for t in range(ref.shape[1]):
+                ref[c, t, 184:208, :] = jnp.zeros((24, LANES), jnp.float32)
+
+    def core_copy(m):
+        return pltpu.make_async_remote_copy(
+            src_ref=smooth.at[:, lanes_of(m)], dst_ref=partner.at[:, lanes_of(m)],
+            send_sem=core_send.at[m], recv_sem=core_recv.at[m],
+            device_id=(slab, core_peer), device_id_type=MESH,
+        )
+
+    def x_copy(m):
+        start = pl.multiple_of((1 - chip) * half_rows, HALF)
+        return pltpu.make_async_remote_copy(
+            src_ref=smooth.at[pl.ds(start, half_rows), lanes_of(m)],
+            dst_ref=across.at[:, lanes_of(m)],
+            send_sem=x_send.at[m], recv_sem=x_recv.at[m],
+            device_id=(slab, x_peer), device_id_type=MESH,
+        )
+
+    def sweep(ref, c, e, r, coef):
+        here = ref[c, e, pl.ds(OFF + r, HALF), :]
+        near = ref[c, e + 1, pl.ds(OFF + r, HALF), :] + ref[c, e - 1, pl.ds(OFF + r, HALF), :]
+        if c + 1 < chans:
+            near = near + ref[c + 1, e, pl.ds(OFF + r, HALF), :]
+        if c > 0:
+            near = near + ref[c - 1, e, pl.ds(OFF + r, HALF), :]
+        near = near + ref[c, e, pl.ds(OFF + r - 1, HALF), :]
+        near = near + ref[c, e, pl.ds(OFF + r + 1, HALF), :]
+        return here + coef * (near - 6.0 * here)
+
+    def chunk(m, carry):
+        @pl.when(slab > 0)
+        def _():
+            halo_up(m).wait_recv()
+
+        @pl.when(slab < 7)
+        def _():
+            halo_down(m).wait_recv()
+
+        lanes = lanes_of(m)
+        for c in range(chans):
+            for e in range(rows + 4):
+                if e < 2:
+                    block = lo[c, e, :, lanes]
+                elif e < rows + 2:
+                    block = bins[c, e - 2, :, lanes]
+                else:
+                    block = hi[c, e - rows - 2, :, lanes]
+                block = block.astype(jnp.float32)
+                f0[c, e, OFF:OFF + phis, :] = block
+                f0[c, e, OFF - 1:OFF, :] = block[phis - 1:phis]
+                f0[c, e, OFF + phis:OFF + phis + 1, :] = block[0:1]
+
+        def first(t, carry):
+            for c in range(chans):
+                for r in (0, HALF):
+                    f1[c, t, pl.ds(OFF + r, HALF), :] = sweep(
+                        f0, c, t + 1, r, diff[c, t, pl.ds(r, HALF), :]
+                    )
+                f1[c, t, OFF - 1:OFF, :] = f1[c, t, OFF + phis - 1:OFF + phis, :]
+                f1[c, t, OFF + phis:OFF + phis + 1, :] = f1[c, t, OFF:OFF + 1, :]
+            return carry
+
+        lax.fori_loop(0, rows + 2, first, 0)
+
+        def second(t, carry):
+            for c in range(chans):
+                for h in range(2):
+                    r = h * HALF
+                    value = sweep(f1, c, t + 1, r, diff[c, t + 1, pl.ds(r, HALF), :])
+                    value = value * mask[t, pl.ds(r, HALF), :]
+                    at = pl.multiple_of(h * half_rows + (c * rows + t) * HALF, HALF)
+                    smooth[pl.ds(at, HALF), lanes] = value.astype(jnp.bfloat16)
+            return carry
+
+        lax.fori_loop(0, rows, second, 0)
+        core_copy(m).start()
+        x_copy(m).start()
+        return carry
+
+    lax.fori_loop(0, n_chunk, chunk, 0)
+
+    def y_copy(k, zz):
+        at, size = SEGS[k]
+        return pltpu.make_async_remote_copy(
+            src_ref=gram.at[pl.ds(pl.multiple_of((2 * zz + 1 - y) * 64, 64), 64), pl.ds(at, size)],
+            dst_ref=ybuf.at[pl.ds(zz * 64, 64), pl.ds(at, size)],
+            send_sem=y_send.at[k, zz], recv_sem=y_recv.at[k, zz],
+            device_id=(2 * z + 1 - y, tile), device_id_type=MESH,
+        )
+
+    def z_copy(k, step):
+        at, size = SEGS[k]
+        zz = lax.rem(z + step, 4)
+        return pltpu.make_async_remote_copy(
+            src_ref=gram.at[pl.ds(pl.multiple_of((2 * zz + y) * 64, 64), 64), pl.ds(at, size)],
+            dst_ref=zbuf.at[step - 1, :, pl.ds(at, size)],
+            send_sem=z_send.at[k, step - 1], recv_sem=z_recv.at[k, step - 1],
+            device_id=(2 * zz + y, tile), device_id_type=MESH,
+        )
+
+    def gather_copy(k, peer, send, recv):
+        at, size = SEGS[k]
+        return pltpu.make_async_remote_copy(
+            src_ref=out.at[tile, :, pl.ds(at, size)], dst_ref=out.at[tile, :, pl.ds(at, size)],
+            send_sem=send.at[k], recv_sem=recv.at[k],
+            device_id=(slab, peer), device_id_type=MESH,
+        )
+
+    def forward_copy(k):
+        at, size = SEGS[k]
+        return pltpu.make_async_remote_copy(
+            src_ref=out.at[x_peer, :, pl.ds(at, size)], dst_ref=out.at[x_peer, :, pl.ds(at, size)],
+            send_sem=gf_send.at[k], recv_sem=gf_recv.at[k],
+            device_id=(slab, core_peer), device_id_type=MESH,
+        )
+
+    def y_start(k):
+        for zz in range(4):
+            y_copy(k, zz).start()
+
+    def y_finish(k):
+        at, size = SEGS[k]
+        for zz in (0, 1, 2, 3):
+            y_copy(k, zz).wait_recv()
+        for zz in range(4):
+            mine = pl.ds(pl.multiple_of((2 * zz + y) * 64, 64), 64)
+            gram[mine, pl.ds(at, size)] += ybuf[pl.ds(zz * 64, 64), pl.ds(at, size)]
+        for step in (2, 1, 3):
+            z_copy(k, step).start()
+
+    def z_finish(k):
+        at, size = SEGS[k]
+        for step in (1, 2, 3):
+            z_copy(k, step).wait_recv()
+        cols = pl.ds(at, size)
+        total = gram[pl.ds(pl.multiple_of(slab * 64, 64), 64), cols]
+        for step in range(3):
+            total = total + zbuf[step, :, cols]
+        out[tile, :, cols] = total * scale
+        gather_copy(k, x_peer, gx_send, gx_recv).start()
+        gather_copy(k, core_peer, g_send, g_recv).start()
+
+    def pair(left, right, at):
+        gram[:, at:at + right.shape[1]] = contract(left[...], right[...])
+
+    def half_of(ref, h):
+        return ref.at[h * half_rows:(h + 1) * half_rows, :]
+
+    own = slice(0, 512)
+    gram[:, own] = contract(half_of(smooth, 0)[...], half_of(smooth, 0)[...])
+    gram[:, own] += contract(half_of(smooth, 1)[...], half_of(smooth, 1)[...])
+    y_start(0)
+    for m in range(n_chunk):
+        core_copy(m).wait_recv()
+    for c in range(2):
+        left, right = (smooth, partner) if c == 0 else (partner, smooth)
+
+        @pl.when(core == c)
+        def _():
+            cols = slice(c * 256, c * 256 + 256)
+            gram[:, 512:768] = contract(left[0:half_rows, :], right[0:half_rows, cols])
+            gram[:, 512:768] += contract(left[half_rows:, :], right[half_rows:, cols])
+    y_start(1)
+    for m in range(n_chunk):
+        x_copy(m).wait_recv()
+    for piece in range(2):
+        for x in range(2):
+            for c in range(2):
+                mine = smooth if piece == c else partner
+
+                @pl.when(tile == 2 * x + c)
+                def _():
+                    if x == 0:
+                        pair(half_of(mine, 0), across, 768 + 512 * piece)
+                    else:
+                        pair(across, half_of(mine, 1), 768 + 512 * piece)
+        y_start(2 + piece)
+    for k in range(4):
+        y_finish(k)
+    for k in range(4):
+        z_finish(k)
+    for k in range(4):
+        gather_copy(k, x_peer, gx_send, gx_recv).wait_recv()
+        forward_copy(k).start()
+    for k in range(4):
+        gather_copy(k, core_peer, g_send, g_recv).wait_recv()
+        forward_copy(k).wait_recv()
+
+    for m in range(n_chunk):
+        @pl.when(slab < 7)
+        def _():
+            halo_up(m).wait_send()
+
+        @pl.when(slab > 0)
+        def _():
+            halo_down(m).wait_send()
+        core_copy(m).wait_send()
+        x_copy(m).wait_send()
+    for k in range(4):
+        for zz in range(4):
+            y_copy(k, zz).wait_send()
+        for step in (1, 2, 3):
+            z_copy(k, step).wait_send()
+        gather_copy(k, x_peer, gx_send, gx_recv).wait_send()
+        gather_copy(k, core_peer, g_send, g_recv).wait_send()
+        forward_copy(k).wait_send()
+
+
+def fused(brdf_bins, diffusion, valid_mask, tile_owner):
+    chans, rows, phis, width = brdf_bins.shape
+    slab = lax.axis_index("slab")
+    my_tile = lax.axis_index("tile")
+    margin = jnp.pad(diffusion, ((0, 0), (1, 1), (0, 2 * HALF - phis)))
+    local = lax.dynamic_slice_in_dim(margin, slab * rows, rows + 2, 1)
+    diff = jnp.broadcast_to(local[..., None], local.shape + (LANES,))
+    mask = jnp.pad(valid_mask.astype(jnp.float32), ((0, 0), (0, 2 * HALF - phis)))
+    mask = jnp.broadcast_to(mask[..., None], mask.shape + (LANES,))
+    scale = 1.0 / math.sqrt(chans * rows * phis * lax.axis_size("slab"))
+    dma = pltpu.SemaphoreType.DMA
+    all_rows = chans * rows * 2 * HALF
+    parts = pl.pallas_call(
+        functools.partial(gram_kernel, scale),
+        out_shape=jax.ShapeDtypeStruct((4, 64, 1792), jnp.float32),
+        in_specs=[pl.BlockSpec(memory_space=pltpu.VMEM)] * 3,
+        out_specs=pl.BlockSpec(memory_space=pltpu.VMEM),
+        scratch_shapes=[
+            pltpu.VMEM((chans, 2, phis, width), jnp.bfloat16),
+            pltpu.VMEM((chans, 2, phis, width), jnp.bfloat16),
+            pltpu.VMEM((chans, rows + 4, 208, LANES), jnp.float32),
+            pltpu.VMEM((chans, rows + 2, 208, LANES), jnp.float32),
+            pltpu.VMEM((all_rows, width), jnp.bfloat16),
+            pltpu.VMEM((all_rows, width), jnp.bfloat16),
+            pltpu.VMEM((all_rows // 2, width), jnp.bfloat16),
+            pltpu.VMEM((512, 1792), jnp.float32),
+            pltpu.VMEM((256, 1792), jnp.float32),
+            pltpu.VMEM((3, 64, 1792), jnp.float32),
+            dma((2, 4)), dma((2, 4)), dma((4,)), dma((4,)), dma((4,)), dma((4,)),
+            dma((4, 4)), dma((4, 4)), dma((4, 3)), dma((4, 3)),
+            dma((4,)), dma((4,)), dma((4,)), dma((4,)), dma((4,)), dma((4,)),
+        ],
+        compiler_params=pltpu.CompilerParams(
+            collective_id=0, has_side_effects=True, vmem_limit_bytes=48 * 1024 * 1024
+        ),
+    )(brdf_bins, diff, mask)
+    own = [parts[t, :, 0:512] for t in range(4)]
+    side = [parts[t, :, 512:768] for t in range(4)]
+    cross = [[parts[t, :, 768 + 512 * p:1280 + 512 * p] for p in range(2)] for t in range(4)]
+    row_tile, col_tile = np.triu_indices(4)
+    tiles = []
+    for i, j in zip(row_tile.tolist(), col_tile.tolist()):
+        if i == j:
+            tiles.append(own[i])
+        elif i // 2 == j // 2:
+            tiles.append(jnp.concatenate([side[i], side[j]], axis=1))
+        else:
+            tiles.append(cross[j - 2][i] + cross[2 + i][j - 2])
+    tiles = jnp.stack(tiles)
+    n_upper = len(row_tile)
+    position = jnp.arange(n_upper, dtype=jnp.int32)
+    before = (tile_owner[None, :] == tile_owner[:, None]) & (position[None, :] < position[:, None])
+    rank_in = jnp.sum(before.astype(jnp.int32), axis=1)
+    cap_slots = 2 * ((n_upper + 3) // 4)
+    slot_ids = jnp.arange(cap_slots, dtype=jnp.int32)
+    chosen = (tile_owner[None, :] == my_tile) & (rank_in[None, :] == slot_ids[:, None])
+    source = jnp.sum(jnp.where(chosen, position[None, :], 0), axis=1).astype(jnp.int32)
+    picked = jnp.take(tiles, source, axis=0)
+    return jnp.where(jnp.any(chosen, axis=1)[:, None, None], picked, 0.0)
+
+
 def solution(mesh):
+    body = fused if (mesh.shape["slab"], mesh.shape["tile"]) == (8, 4) else on_device
     in_specs = (P(None, "slab", None, "tile"), P(), P("slab", None), P())
     out_specs = P("tile", "slab", None)
     return jax.shard_map(
-        on_device, mesh=mesh, in_specs=in_specs, out_specs=out_specs, check_vma=False
+        body, mesh=mesh, in_specs=in_specs, out_specs=out_specs, check_vma=False
     )

time: 339 us -> 125 us (0.37); the launches traced: 335 us -> 125 us
  waiting for transfers between devices: 230 us -> 0 us
  Pallas kernels: 0 us -> 120 us
  local copies, waits for them, and re-layouts: 40.6 us -> 2.74 us
  other arithmetic: 29.9 us -> 1.61 us
  between operations: 13.5 us -> 0.17 us
  matrix products: 11.1 us -> 0 us
  starting transfers between devices: 9.69 us -> 0 us
    pallas_call x0 -> x1, Pallas kernels: none -> 120 us  [fused(): pl.pallas_call(functools.partial(gram_kernel, scale), out_shape=jax.Shape...]
    reduce_scatter x1 -> x0, waiting for transfers between devices: 88.1 us -> none  [on_device(): lax.psum_scatter(tile_slots, 'slab', scatter_dimension=1, tiled=True)]
    all_gather x1 -> x0, waiting for transfers between devices: 75.6 us -> none  [on_device(): lax.all_gather(flat_rows, 'tile', axis=1, tiled=True)]
    ppermute x2 -> x0, waiting for transfers between devices: 43.4 us -> none  [the longest x1 43.4 us: padded_2(): lax.ppermute(tail, axis, [(i, (i + 1) % count) for i in range(ends)])]
    slice x7 -> x0, local copies, waits for them, and re-layouts: 27 us -> none  [the longest x3 17.1 us: stencil(): neighbours = neighbours + jnp.roll(center, 1, 2) + jnp.roll(center, -1, 2)]
    all_to_all x1 -> x0, waiting for transfers between devices: 23.3 us -> none  [on_device(): lax.all_to_all(outgoing, 'tile', split_axis=0, concat_axis=0, tiled=True)]
    add x1 -> x0, other arithmetic: 14.4 us -> none  [stencil(): return center + diffusion_rows[..., None] * (neighbours - 6.0 * center)]
    dot_general x1 -> x0, matrix products: 11.1 us -> none  [contract_rows(): lax.dot_general(left_cols, right_cols, (((0,), (0,)), ((), ())), preferre...]
  transfers between devices with their start and end apart: 5 -> 0, of which waited for: 4 -> 0; matrix products, arithmetic and copies ran while one was open for 2% -> 0% of each run, Pallas kernels for 0% -> 0%
where the time goes in v1:
time: 125 us
  Pallas kernels  120 us (96%)
  local copies, waits for them, and re-layouts  2.74 us (2%)
  other arithmetic  1.61 us (1%)
    pallas_call x1, Pallas kernels, fused(): pl.pallas_call(functools.partial(gram_kernel, scale), out_shape=jax.Shape...  120 us

profile of v1, /device:TPU:23, one launch (start us, length us, event | category | flops | bytes accessed | tf_op | source)
XLA Modules:
  0.0 124.9 jit_solution(16940341448764281862)
XLA Ops:
  0.0 0.0 copy-start
  0.0 0.8 pad_dynamic-slice_fusion
  0.8 0.6 broadcast_in_dim.59.diff
  1.4 0.0 copy-done
  1.5 0.2 broadcast_in_dim.60.mask
  1.6 120.4 %shard_map.46 = f32[4,64,1792]{2,1,0:T(8,128)S(1)} custom-call(bf16[3,5,180,512]{3,2,1,0:T(8,128)(2,1)} %bins.1, f32[3,7,192,128]{3,2,1,0:T(8,128)S(1)} %broadcast_in_dim.59.diff, f32[5,192,128]{2,1,0:T(8,128)S(1)} %broadcast_in_dim.60.mask), custom_call_target="tpu_custom_call" | custom-call | tf_op jit(solution)/shard_map/pallas_call | solution.py:394
  122.1 0.0 copy-start.1
  122.3 0.5 copy-done.1
  122.7 0.2 convert_reduce_fusion
  122.9 0.1 select_reduce_fusion
  123.1 0.6 gather_fusion
  123.7 0.1 fusion.4
  123.8 1.1 select_select_fusion
  (17 shorter events, 0.2 us)
Async XLA Ops:
  0.0 1.4 %copy-start = (s32[5,180]{1,0:T(8,128)S(1)}, s32[5,180]{1,0:T(8,128)}, u32[]{:S(2)}) copy-start(s32[5,180]{1,0:T(8,128)} %param.6) | copy-start | bytes 10804
  122.1 0.7 copy-start.1

commit v2 on v1

--- a/solution.py
+++ b/solution.py
@@ -96,6 +96,8 @@
 LANES = 128
 HALF = 96
 OFF = 8
+DEPTH = 2
+LEVELS = 32767.0
 SEGS = ((0, 512), (512, 256), (768, 512), (1280, 512))
 
 
@@ -105,9 +107,21 @@
     )
 
 
+def coded(block):
+    peak = jnp.maximum(jnp.max(jnp.abs(block), axis=0, keepdims=True), 1e-30)
+    code = jnp.round(block * (LEVELS / peak)).astype(jnp.int32).astype(jnp.int16)
+    return code, peak * (1.0 / LEVELS)
+
+
+def decoded(code, unit):
+    return code.astype(jnp.int32).astype(jnp.float32) * unit
+
+
 def gram_kernel(
-    scale, bins, diff, mask, out, lo, hi, f0, f1, smooth, partner, across, gram, ybuf, zbuf,
-    halo_send, halo_recv, core_send, core_recv, x_send, x_recv, y_send, y_recv, z_send, z_recv,
+    scale, bins, diff, mask, out, lo, hi, f0, f1, smooth, partner, across, gram,
+    yout, ybuf, youtu, ybufu, zout, zbuf, zoutu, zbufu,
+    halo_send, halo_recv, core_send, core_recv, x_send, x_recv, y_send, y_recv, yu_send, yu_recv,
+    z_send, z_recv, zu_send, zu_recv,
     g_send, g_recv, gx_send, gx_recv, gf_send, gf_recv,
 ):
     slab = lax.axis_index("slab")
@@ -151,7 +165,7 @@
             device_id=(jnp.maximum(slab - 1, 0), tile), device_id_type=MESH,
         )
 
-    for m in range(n_chunk):
+    def halo_start(m):
         @pl.when(slab < 7)
         def _():
             halo_up(m).start()
@@ -159,6 +173,9 @@
         @pl.when(slab > 0)
         def _():
             halo_down(m).start()
+
+    for m in range(DEPTH):
+        halo_start(m)
 
     @pl.when(slab == 0)
     def _():
@@ -208,6 +225,18 @@
         @pl.when(slab < 7)
         def _():
             halo_down(m).wait_recv()
+
+        @pl.when(slab < 7)
+        def _():
+            halo_up(m).wait_send()
+
+        @pl.when(slab > 0)
+        def _():
+            halo_down(m).wait_send()
+
+        @pl.when(m + DEPTH < n_chunk)
+        def _():
+            halo_start(m + DEPTH)
 
         lanes = lanes_of(m)
         for c in range(chans):
@@ -252,24 +281,35 @@
 
     lax.fori_loop(0, n_chunk, chunk, 0)
 
-    def y_copy(k, zz):
-        at, size = SEGS[k]
-        return pltpu.make_async_remote_copy(
-            src_ref=gram.at[pl.ds(pl.multiple_of((2 * zz + 1 - y) * 64, 64), 64), pl.ds(at, size)],
-            dst_ref=ybuf.at[pl.ds(zz * 64, 64), pl.ds(at, size)],
-            send_sem=y_send.at[k, zz], recv_sem=y_recv.at[k, zz],
-            device_id=(2 * z + 1 - y, tile), device_id_type=MESH,
-        )
-
-    def z_copy(k, step):
-        at, size = SEGS[k]
+    def y_copies(k):
+        at, size = SEGS[k]
+        cols = pl.ds(at, size)
+        return [
+            pltpu.make_async_remote_copy(
+                src_ref=src.at[:, cols] if src.ndim == 2 else src.at[:, :, cols],
+                dst_ref=dst.at[:, cols] if src.ndim == 2 else dst.at[:, :, cols],
+                send_sem=send.at[k], recv_sem=recv.at[k],
+                device_id=(2 * z + 1 - y, tile), device_id_type=MESH,
+            )
+            for src, dst, send, recv in (
+                (yout, ybuf, y_send, y_recv), (youtu, ybufu, yu_send, yu_recv)
+            )
+        ]
+
+    def z_copies(k, step):
+        at, size = SEGS[k]
+        cols = pl.ds(at, size)
         zz = lax.rem(z + step, 4)
-        return pltpu.make_async_remote_copy(
-            src_ref=gram.at[pl.ds(pl.multiple_of((2 * zz + y) * 64, 64), 64), pl.ds(at, size)],
-            dst_ref=zbuf.at[step - 1, :, pl.ds(at, size)],
-            send_sem=z_send.at[k, step - 1], recv_sem=z_recv.at[k, step - 1],
-            device_id=(2 * zz + y, tile), device_id_type=MESH,
-        )
+        return [
+            pltpu.make_async_remote_copy(
+                src_ref=src.at[step - 1, :, cols], dst_ref=dst.at[step - 1, :, cols],
+                send_sem=send.at[k, step - 1], recv_sem=recv.at[k, step - 1],
+                device_id=(2 * zz + y, tile), device_id_type=MESH,
+            )
+            for src, dst, send, recv in (
+                (zout, zbuf, z_send, z_recv), (zoutu, zbufu, zu_send, zu_recv)
+            )
+        ]
 
     def gather_copy(k, peer, send, recv):
         at, size = SEGS[k]
@@ -287,28 +327,44 @@
             device_id=(slab, core_peer), device_id_type=MESH,
         )
 
+    def gram_rows(block):
+        return pl.ds(pl.multiple_of(block * 64, 64), 64)
+
     def y_start(k):
+        at, size = SEGS[k]
+        cols = pl.ds(at, size)
         for zz in range(4):
-            y_copy(k, zz).start()
+            code, unit = coded(gram[gram_rows(2 * zz + 1 - y), cols])
+            yout[pl.ds(zz * 64, 64), cols] = code
+            youtu[zz, :, cols] = unit
+        for copy in y_copies(k):
+            copy.start()
 
     def y_finish(k):
         at, size = SEGS[k]
-        for zz in (0, 1, 2, 3):
-            y_copy(k, zz).wait_recv()
+        cols = pl.ds(at, size)
+        for copy in y_copies(k):
+            copy.wait_recv()
         for zz in range(4):
-            mine = pl.ds(pl.multiple_of((2 * zz + y) * 64, 64), 64)
-            gram[mine, pl.ds(at, size)] += ybuf[pl.ds(zz * 64, 64), pl.ds(at, size)]
+            gram[gram_rows(2 * zz + y), cols] += decoded(
+                ybuf[pl.ds(zz * 64, 64), cols], ybufu[zz, :, cols]
+            )
         for step in (2, 1, 3):
-            z_copy(k, step).start()
+            code, unit = coded(gram[gram_rows(2 * lax.rem(z + step, 4) + y), cols])
+            zout[step - 1, :, cols] = code
+            zoutu[step - 1, :, cols] = unit
+            for copy in z_copies(k, step):
+                copy.start()
 
     def z_finish(k):
         at, size = SEGS[k]
         for step in (1, 2, 3):
-            z_copy(k, step).wait_recv()
+            for copy in z_copies(k, step):
+                copy.wait_recv()
         cols = pl.ds(at, size)
         total = gram[pl.ds(pl.multiple_of(slab * 64, 64), 64), cols]
         for step in range(3):
-            total = total + zbuf[step, :, cols]
+            total = total + decoded(zbuf[step, :, cols], zbufu[step, :, cols])
         out[tile, :, cols] = total * scale
         gather_copy(k, x_peer, gx_send, gx_recv).start()
         gather_copy(k, core_peer, g_send, g_recv).start()
@@ -360,20 +416,14 @@
         forward_copy(k).wait_recv()
 
     for m in range(n_chunk):
-        @pl.when(slab < 7)
-        def _():
-            halo_up(m).wait_send()
-
-        @pl.when(slab > 0)
-        def _():
-            halo_down(m).wait_send()
         core_copy(m).wait_send()
         x_copy(m).wait_send()
     for k in range(4):
-        for zz in range(4):
-            y_copy(k, zz).wait_send()
+        for copy in y_copies(k):
+            copy.wait_send()
         for step in (1, 2, 3):
-            z_copy(k, step).wait_send()
+            for copy in z_copies(k, step):
+                copy.wait_send()
         gather_copy(k, x_peer, gx_send, gx_recv).wait_send()
         gather_copy(k, core_peer, g_send, g_recv).wait_send()
         forward_copy(k).wait_send()
@@ -405,10 +455,17 @@
             pltpu.VMEM((all_rows, width), jnp.bfloat16),
             pltpu.VMEM((all_rows // 2, width), jnp.bfloat16),
             pltpu.VMEM((512, 1792), jnp.float32),
-            pltpu.VMEM((256, 1792), jnp.float32),
-            pltpu.VMEM((3, 64, 1792), jnp.float32),
+            pltpu.VMEM((256, 1792), jnp.int16),
+            pltpu.VMEM((256, 1792), jnp.int16),
+            pltpu.VMEM((4, 1, 1792), jnp.float32),
+            pltpu.VMEM((4, 1, 1792), jnp.float32),
+            pltpu.VMEM((3, 64, 1792), jnp.int16),
+            pltpu.VMEM((3, 64, 1792), jnp.int16),
+            pltpu.VMEM((3, 1, 1792), jnp.float32),
+            pltpu.VMEM((3, 1, 1792), jnp.float32),
             dma((2, 4)), dma((2, 4)), dma((4,)), dma((4,)), dma((4,)), dma((4,)),
-            dma((4, 4)), dma((4, 4)), dma((4, 3)), dma((4, 3)),
+            dma((4,)), dma((4,)), dma((4,)), dma((4,)),
+            dma((4, 3)), dma((4, 3)), dma((4, 3)), dma((4, 3)),
             dma((4,)), dma((4,)), dma((4,)), dma((4,)), dma((4,)), dma((4,)),
         ],
         compiler_params=pltpu.CompilerParams(

time: 125 us -> 104 us (0.83)
  Pallas kernels: 120 us -> 98.8 us
    pallas_call x1, Pallas kernels: 120 us -> 98.8 us  [fused(): pl.pallas_call(functools.partial(gram_kernel, scale), out_shape=jax.Shape...]
where the time goes in v2:
time: 104 us; the launch traced here: 103 us
  Pallas kernels  98.8 us (95%)
  local copies, waits for them, and re-layouts  2.74 us (3%)
  other arithmetic  1.61 us (2%)
    pallas_call x1, Pallas kernels, fused(): pl.pallas_call(functools.partial(gram_kernel, scale), out_shape=jax.Shape...  98.8 us

profile of v2, /device:TPU:23, one launch (start us, length us, event | category | flops | bytes accessed | tf_op | source)
XLA Modules:
  0.0 103.4 jit_solution(5345530377635938822)
XLA Ops:
  0.0 0.0 copy-start
  0.0 0.8 pad_dynamic-slice_fusion
  0.8 0.6 broadcast_in_dim.59.diff
  1.4 0.0 copy-done
  1.5 0.2 broadcast_in_dim.60.mask
  1.6 98.8 %shard_map.46 = f32[4,64,1792]{2,1,0:T(8,128)S(1)} custom-call(bf16[3,5,180,512]{3,2,1,0:T(8,128)(2,1)} %bins.1, f32[3,7,192,128]{3,2,1,0:T(8,128)S(1)} %broadcast_in_dim.59.diff, f32[5,192,128]{2,1,0:T(8,128)S(1)} %broadcast_in_dim.60.mask), custom_call_target="tpu_custom_call" | custom-call | tf_op jit(solution)/shard_map/pallas_call | solution.py:444
  100.6 0.0 copy-start.1
  100.8 0.5 copy-done.1
  101.2 0.2 convert_reduce_fusion
  101.4 0.1 select_reduce_fusion
  101.6 0.6 gather_fusion
  102.2 0.1 fusion.4
  102.3 1.1 %select_select_fusion = f32[6,64,512]{2,1,0:T(8,128)} fusion(f32[6,64,512]{2,1,0:T(8,128)S(1)} %gather_fusion, pred[6]{0:T(512)(128)(4,1)S(1)} %compare_and_fusion, pred[6]{0:T(512)(128)(4,1)S(1)} %fusion.4), kind=kLoop, calls=%fused_computation.1 | loop fusion | flops 393216 | bytes 1572876 | tf_op jit(solution)/shard_map/jit(_where)/select_n | solution.py:497
  (17 shorter events, 0.2 us)
Async XLA Ops:
  0.0 1.4 %copy-start = (s32[5,180]{1,0:T(8,128)S(1)}, s32[5,180]{1,0:T(8,128)}, u32[]{:S(2)}) copy-start(s32[5,180]{1,0:T(8,128)} %param.6) | copy-start | bytes 10804
  100.6 0.7 copy-start.1

commit v3 on v2

--- a/solution.py
+++ b/solution.py
@@ -118,9 +118,9 @@
 
 
 def gram_kernel(
-    scale, bins, diff, mask, out, lo, hi, f0, f1, smooth, partner, across, gram,
+    scale, bins, diff, mask, out, lo, hi, relay, f0, f1, smooth, partner, across, gram,
     yout, ybuf, youtu, ybufu, zout, zbuf, zoutu, zbufu,
-    halo_send, halo_recv, core_send, core_recv, x_send, x_recv, y_send, y_recv, yu_send, yu_recv,
+    halo_send, halo_recv, relay_send, relay_recv, core_send, core_recv, x_send, x_recv, y_send, y_recv, yu_send, yu_recv,
     z_send, z_recv, zu_send, zu_recv,
     g_send, g_recv, gx_send, gx_recv, gf_send, gf_recv,
 ):
@@ -165,17 +165,84 @@
             device_id=(jnp.maximum(slab - 1, 0), tile), device_id_type=MESH,
         )
 
+    up_far = (y == 1) & (z < 3)
+    down_far = (y == 0) & (z > 0)
+    up_relay = (y == 1) & (z > 0)
+    down_relay = (y == 0) & (z < 3)
+
+    def up_detour(m):
+        return up_far & (m >= 3 - z)
+
+    def down_detour(m):
+        return down_far & (m >= z)
+
+    def up_passes(m):
+        return up_relay & (m >= 4 - z)
+
+    def down_passes(m):
+        return down_relay & (m >= z + 1)
+
+    def hop(m, start, sem, target):
+        return pltpu.make_async_remote_copy(
+            src_ref=bins.at[:, pl.ds(start, 2), :, lanes_of(m)],
+            dst_ref=relay.at[:, :, :, lanes_of(m)],
+            send_sem=halo_send.at[sem, m], recv_sem=relay_recv.at[m],
+            device_id=(target, tile), device_id_type=MESH,
+        )
+
+    def passed(m, sem, target):
+        return pltpu.make_async_remote_copy(
+            src_ref=relay.at[:, :, :, lanes_of(m)],
+            dst_ref=(lo, hi)[sem].at[:, :, :, lanes_of(m)],
+            send_sem=relay_send.at[m], recv_sem=halo_recv.at[sem, m],
+            device_id=(target, tile), device_id_type=MESH,
+        )
+
+    def hop_up(m):
+        return hop(m, rows - 2, 0, jnp.minimum(slab + 2, 7))
+
+    def hop_down(m):
+        return hop(m, 0, 1, jnp.maximum(slab - 2, 0))
+
+    def pass_up(m):
+        return passed(m, 0, jnp.maximum(slab - 1, 0))
+
+    def pass_down(m):
+        return passed(m, 1, jnp.minimum(slab + 1, 7))
+
     def halo_start(m):
-        @pl.when(slab < 7)
+        @pl.when((slab < 7) & jnp.logical_not(up_detour(m)))
         def _():
             halo_up(m).start()
 
-        @pl.when(slab > 0)
+        @pl.when((slab > 0) & jnp.logical_not(down_detour(m)))
         def _():
             halo_down(m).start()
+
+    def hop_start(m):
+        @pl.when(up_detour(m))
+        def _():
+            hop_up(m).start()
+
+        @pl.when(down_detour(m))
+        def _():
+            hop_down(m).start()
+
+    def relay_pass(m):
+        @pl.when(up_passes(m))
+        def _():
+            hop_up(m).wait_recv()
+            pass_up(m).start()
+
+        @pl.when(down_passes(m))
+        def _():
+            hop_down(m).wait_recv()
+            pass_down(m).start()
 
     for m in range(DEPTH):
         halo_start(m)
+    for m in range(1, n_chunk):
+        hop_start(m)
 
     @pl.when(slab == 0)
     def _():
@@ -189,6 +256,9 @@
         for c in range(ref.shape[0]):
             for t in range(ref.shape[1]):
                 ref[c, t, 184:208, :] = jnp.zeros((24, LANES), jnp.float32)
+
+    for m in range(1, DEPTH):
+        relay_pass(m)
 
     def core_copy(m):
         return pltpu.make_async_remote_copy(
@@ -237,6 +307,7 @@
         @pl.when(m + DEPTH < n_chunk)
         def _():
             halo_start(m + DEPTH)
+            relay_pass(m + DEPTH)
 
         lanes = lanes_of(m)
         for c in range(chans):
@@ -404,18 +475,34 @@
                     else:
                         pair(across, half_of(mine, 1), 768 + 512 * piece)
         y_start(2 + piece)
-    for k in range(4):
-        y_finish(k)
-    for k in range(4):
-        z_finish(k)
-    for k in range(4):
+    def forward(k):
         gather_copy(k, x_peer, gx_send, gx_recv).wait_recv()
         forward_copy(k).start()
+
+    y_finish(0)
+    y_finish(1)
+    z_finish(0)
+    y_finish(2)
+    z_finish(1)
+    y_finish(3)
+    forward(0)
+    z_finish(2)
+    forward(1)
+    z_finish(3)
+    forward(2)
+    forward(3)
     for k in range(4):
         gather_copy(k, core_peer, g_send, g_recv).wait_recv()
         forward_copy(k).wait_recv()
 
     for m in range(n_chunk):
+        @pl.when(up_passes(m))
+        def _():
+            pass_up(m).wait_send()
+
+        @pl.when(down_passes(m))
+        def _():
+            pass_down(m).wait_send()
         core_copy(m).wait_send()
         x_copy(m).wait_send()
     for k in range(4):
@@ -449,6 +536,7 @@
         scratch_shapes=[
             pltpu.VMEM((chans, 2, phis, width), jnp.bfloat16),
             pltpu.VMEM((chans, 2, phis, width), jnp.bfloat16),
+            pltpu.VMEM((chans, 2, phis, width), jnp.bfloat16),
             pltpu.VMEM((chans, rows + 4, 208, LANES), jnp.float32),
             pltpu.VMEM((chans, rows + 2, 208, LANES), jnp.float32),
             pltpu.VMEM((all_rows, width), jnp.bfloat16),
@@ -463,7 +551,7 @@
             pltpu.VMEM((3, 64, 1792), jnp.int16),
             pltpu.VMEM((3, 1, 1792), jnp.float32),
             pltpu.VMEM((3, 1, 1792), jnp.float32),
-            dma((2, 4)), dma((2, 4)), dma((4,)), dma((4,)), dma((4,)), dma((4,)),
+            dma((2, 4)), dma((2, 4)), dma((4,)), dma((4,)), dma((4,)), dma((4,)), dma((4,)), dma((4,)),
             dma((4,)), dma((4,)), dma((4,)), dma((4,)),
             dma((4, 3)), dma((4, 3)), dma((4, 3)), dma((4, 3)),
             dma((4,)), dma((4,)), dma((4,)), dma((4,)), dma((4,)), dma((4,)),

time: 104 us -> 102 us (0.981)
  Pallas kernels: 98.8 us -> 97.1 us
    pallas_call x1, Pallas kernels: 98.8 us -> 97.1 us  [fused(): pl.pallas_call(functools.partial(gram_kernel, scale), out_shape=jax.Shape...]
where the time goes in v3:
time: 102 us
  Pallas kernels  97.1 us (95%)
  local copies, waits for them, and re-layouts  2.74 us (3%)
  other arithmetic  1.61 us (2%)
    pallas_call x1, Pallas kernels, fused(): pl.pallas_call(functools.partial(gram_kernel, scale), out_shape=jax.Shape...  97.1 us

profile of v3, /device:TPU:23, one launch (start us, length us, event | category | flops | bytes accessed | tf_op | source)
XLA Modules:
  0.0 101.6 jit_solution(15260164170456482959)
XLA Ops:
  0.0 0.0 copy-start
  0.0 0.8 pad_dynamic-slice_fusion
  0.8 0.6 broadcast_in_dim.59.diff
  1.4 0.0 copy-done
  1.5 0.2 broadcast_in_dim.60.mask
  1.6 97.1 %shard_map.46 = f32[4,64,1792]{2,1,0:T(8,128)S(1)} custom-call(bf16[3,5,180,512]{3,2,1,0:T(8,128)(2,1)} %bins.1, f32[3,7,192,128]{3,2,1,0:T(8,128)S(1)} %broadcast_in_dim.59.diff, f32[5,192,128]{2,1,0:T(8,128)S(1)} %broadcast_in_dim.60.mask), custom_call_target="tpu_custom_call" | custom-call | tf_op jit(solution)/shard_map/pallas_call | solution.py:531
  98.8 0.0 copy-start.1
  99.0 0.5 copy-done.1
  99.5 0.2 convert_reduce_fusion
  99.7 0.1 select_reduce_fusion
  99.8 0.6 gather_fusion
  100.4 0.1 fusion.4
  100.6 1.1 %select_select_fusion = f32[6,64,512]{2,1,0:T(8,128)} fusion(f32[6,64,512]{2,1,0:T(8,128)S(1)} %gather_fusion, pred[6]{0:T(512)(128)(4,1)S(1)} %compare_and_fusion, pred[6]{0:T(512)(128)(4,1)S(1)} %fusion.4), kind=kLoop, calls=%fused_computation.1 | loop fusion | flops 393216 | bytes 1572876 | tf_op jit(solution)/shard_map/jit(_where)/select_n | solution.py:585
  (17 shorter events, 0.2 us)
Async XLA Ops:
  0.0 1.4 %copy-start = (s32[5,180]{1,0:T(8,128)S(1)}, s32[5,180]{1,0:T(8,128)}, u32[]{:S(2)}) copy-start(s32[5,180]{1,0:T(8,128)} %param.6) | copy-start | bytes 10804
  98.8 0.7 copy-start.1

commit v4 on v3

--- a/solution.py
+++ b/solution.py
@@ -119,10 +119,11 @@
 
 def gram_kernel(
     scale, bins, diff, mask, out, lo, hi, relay, f0, f1, smooth, partner, across, gram,
-    yout, ybuf, youtu, ybufu, zout, zbuf, zoutu, zbufu,
+    yout, ybuf, youtu, ybufu, zout, zbuf, zoutu, zbufu, gcode, gunit,
     halo_send, halo_recv, relay_send, relay_recv, core_send, core_recv, x_send, x_recv, y_send, y_recv, yu_send, yu_recv,
     z_send, z_recv, zu_send, zu_recv,
     g_send, g_recv, gx_send, gx_recv, gf_send, gf_recv,
+    gu_send, gu_recv, gxu_send, gxu_recv, gfu_send, gfu_recv,
 ):
     slab = lax.axis_index("slab")
     tile = lax.axis_index("tile")
@@ -382,21 +383,32 @@
             )
         ]
 
-    def gather_copy(k, peer, send, recv):
+    def shared(k, source, peer, sems):
         at, size = SEGS[k]
-        return pltpu.make_async_remote_copy(
-            src_ref=out.at[tile, :, pl.ds(at, size)], dst_ref=out.at[tile, :, pl.ds(at, size)],
-            send_sem=send.at[k], recv_sem=recv.at[k],
-            device_id=(slab, peer), device_id_type=MESH,
-        )
-
-    def forward_copy(k):
+        cols = pl.ds(at, size)
+        return [
+            pltpu.make_async_remote_copy(
+                src_ref=ref.at[source, :, cols], dst_ref=ref.at[source, :, cols],
+                send_sem=sems[2 * n].at[k], recv_sem=sems[2 * n + 1].at[k],
+                device_id=(slab, peer), device_id_type=MESH,
+            )
+            for n, ref in enumerate((gcode, gunit))
+        ]
+
+    core_sems = (g_send, g_recv, gu_send, gu_recv)
+    across_sems = (gx_send, gx_recv, gxu_send, gxu_recv)
+    forward_sems = (gf_send, gf_recv, gfu_send, gfu_recv)
+
+    def gathers(k):
+        return shared(k, tile, x_peer, across_sems) + shared(k, tile, core_peer, core_sems)
+
+    def forwards(k):
+        return shared(k, x_peer, core_peer, forward_sems)
+
+    def decode_from(k, source):
         at, size = SEGS[k]
-        return pltpu.make_async_remote_copy(
-            src_ref=out.at[x_peer, :, pl.ds(at, size)], dst_ref=out.at[x_peer, :, pl.ds(at, size)],
-            send_sem=gf_send.at[k], recv_sem=gf_recv.at[k],
-            device_id=(slab, core_peer), device_id_type=MESH,
-        )
+        cols = pl.ds(at, size)
+        out[source, :, cols] = decoded(gcode[source, :, cols], gunit[source, :, cols])
 
     def gram_rows(block):
         return pl.ds(pl.multiple_of(block * 64, 64), 64)
@@ -436,9 +448,13 @@
         total = gram[pl.ds(pl.multiple_of(slab * 64, 64), 64), cols]
         for step in range(3):
             total = total + decoded(zbuf[step, :, cols], zbufu[step, :, cols])
-        out[tile, :, cols] = total * scale
-        gather_copy(k, x_peer, gx_send, gx_recv).start()
-        gather_copy(k, core_peer, g_send, g_recv).start()
+        total = total * scale
+        code, unit = coded(total)
+        gcode[tile, :, cols] = code
+        gunit[tile, :, cols] = unit
+        for copy in gathers(k):
+            copy.start()
+        out[tile, :, cols] = total
 
     def pair(left, right, at):
         gram[:, at:at + right.shape[1]] = contract(left[...], right[...])
@@ -476,8 +492,11 @@
                         pair(across, half_of(mine, 1), 768 + 512 * piece)
         y_start(2 + piece)
     def forward(k):
-        gather_copy(k, x_peer, gx_send, gx_recv).wait_recv()
-        forward_copy(k).start()
+        for copy in shared(k, tile, x_peer, across_sems):
+            copy.wait_recv()
+        for copy in forwards(k):
+            copy.start()
+        decode_from(k, x_peer)
 
     y_finish(0)
     y_finish(1)
@@ -492,8 +511,13 @@
     forward(2)
     forward(3)
     for k in range(4):
-        gather_copy(k, core_peer, g_send, g_recv).wait_recv()
-        forward_copy(k).wait_recv()
+        for copy in shared(k, tile, core_peer, core_sems):
+            copy.wait_recv()
+        decode_from(k, core_peer)
+    for k in range(4):
+        for copy in forwards(k):
+            copy.wait_recv()
+        decode_from(k, lax.rem(core_peer + 2, 4))
 
     for m in range(n_chunk):
         @pl.when(up_passes(m))
@@ -511,9 +535,8 @@
         for step in (1, 2, 3):
             for copy in z_copies(k, step):
                 copy.wait_send()
-        gather_copy(k, x_peer, gx_send, gx_recv).wait_send()
-        gather_copy(k, core_peer, g_send, g_recv).wait_send()
-        forward_copy(k).wait_send()
+        for copy in gathers(k) + forwards(k):
+            copy.wait_send()
 
 
 def fused(brdf_bins, diffusion, valid_mask, tile_owner):
@@ -551,9 +574,12 @@
             pltpu.VMEM((3, 64, 1792), jnp.int16),
             pltpu.VMEM((3, 1, 1792), jnp.float32),
             pltpu.VMEM((3, 1, 1792), jnp.float32),
+            pltpu.VMEM((4, 64, 1792), jnp.int16),
+            pltpu.VMEM((4, 1, 1792), jnp.float32),
             dma((2, 4)), dma((2, 4)), dma((4,)), dma((4,)), dma((4,)), dma((4,)), dma((4,)), dma((4,)),
             dma((4,)), dma((4,)), dma((4,)), dma((4,)),
             dma((4, 3)), dma((4, 3)), dma((4, 3)), dma((4, 3)),
+            dma((4,)), dma((4,)), dma((4,)), dma((4,)), dma((4,)), dma((4,)),
             dma((4,)), dma((4,)), dma((4,)), dma((4,)), dma((4,)), dma((4,)),
         ],
         compiler_params=pltpu.CompilerParams(

time: 102 us -> 101 us (level)
  Pallas kernels: 97.1 us -> 95.8 us
    pallas_call x1, Pallas kernels: 97.1 us -> 95.8 us  [fused(): pl.pallas_call(functools.partial(gram_kernel, scale), out_shape=jax.Shape...]
where the time goes in v4:
time: 101 us; the launch traced here: 100 us
  Pallas kernels  95.8 us (95%)
  local copies, waits for them, and re-layouts  2.74 us (3%)
  other arithmetic  1.61 us (2%)
    pallas_call x1, Pallas kernels, fused(): pl.pallas_call(functools.partial(gram_kernel, scale), out_shape=jax.Shape...  95.8 us

profile of v4, /device:TPU:23, one launch (start us, length us, event | category | flops | bytes accessed | tf_op | source)
XLA Modules:
  0.0 100.3 jit_solution(12732285472373188826)
XLA Ops:
  0.0 0.0 copy-start
  0.0 0.8 pad_dynamic-slice_fusion
  0.8 0.6 broadcast_in_dim.59.diff
  1.4 0.0 copy-done
  1.5 0.2 broadcast_in_dim.60.mask
  1.6 95.8 %shard_map.46 = f32[4,64,1792]{2,1,0:T(8,128)S(1)} custom-call(bf16[3,5,180,512]{3,2,1,0:T(8,128)(2,1)} %bins.1, f32[3,7,192,128]{3,2,1,0:T(8,128)S(1)} %broadcast_in_dim.59.diff, f32[5,192,128]{2,1,0:T(8,128)S(1)} %broadcast_in_dim.60.mask), custom_call_target="tpu_custom_call" | custom-call | tf_op jit(solution)/shard_map/pallas_call | solution.py:554
  97.5 0.0 copy-start.1
  97.7 0.5 copy-done.1
  98.2 0.2 convert_reduce_fusion
  98.4 0.1 select_reduce_fusion
  98.5 0.6 gather_fusion
  99.1 0.1 fusion.4
  99.3 1.1 %select_select_fusion = f32[6,64,512]{2,1,0:T(8,128)} fusion(f32[6,64,512]{2,1,0:T(8,128)S(1)} %gather_fusion, pred[6]{0:T(512)(128)(4,1)S(1)} %compare_and_fusion, pred[6]{0:T(512)(128)(4,1)S(1)} %fusion.4), kind=kLoop, calls=%fused_computation.1 | loop fusion | flops 393216 | bytes 1572876 | tf_op jit(solution)/shard_map/jit(_where)/select_n | solution.py:611
  (17 shorter events, 0.2 us)
Async XLA Ops:
  0.0 1.4 %copy-start = (s32[5,180]{1,0:T(8,128)S(1)}, s32[5,180]{1,0:T(8,128)}, u32[]{:S(2)}) copy-start(s32[5,180]{1,0:T(8,128)} %param.6) | copy-start | bytes 10804
  97.5 0.7 copy-start.1
